TPU v7x, 512 devices: a whole 4x4x16 slice. The times are simulated.
512 devices in a mesh: wide: 128 (over y, x, z_lo), sub: 4 (over z_hi, core).
Axes of the slice: x: 4, y: 4, z: 16 (z_hi: 2, z_lo: 8; z = z_hi * 8 + z_lo), core: 2. Of those that a mesh axis runs over, the one named last changes fastest.
Arguments:
- spectrum: float32 [1152, 65536], P(None, ('wide', 'sub')), may hold values from 0.1 to 2
- wind_speed: float32 [65536], P(('wide', 'sub')), may hold values from 5 to 40
- wind_dir: float32 [65536], P(('wide', 'sub')), may hold values from -3.140625 to 3.140625
- wet_mask: int32 [512, 128], P('sub'), may hold values 0 or 1
- row_block: int32 [4, 128], P('sub'), may hold values from 0 to 127, each once within a row
- plus_index: int32 [1152], replicated, may hold values from 0 to 1151, as said below
- minus_index: int32 [1152], replicated, may hold values from 0 to 1151, as said below
Outputs:
- final_spectrum: float32 [1152, 65536], P(None, ('wide', 'sub'))
Inputs may be any that keep to these rules, and one draw needn't show every extreme that they name: plus_index[b] names a bin 1 or 2 frequencies higher, direction turned 1 to 3 steps up; at the highest frequency it is b itself. minus_index[b] names a bin 1 or 2 frequencies lower, direction turned 1 to 3 steps down; at the lowest frequency it is b itself. Each row of row_block is a permutation.
All inputs are finite; a program needn't handle non-finite values. No bound on the sum of `wet_mask` on one device may be relied on, other than what follows from the above.
Results may differ from a plain program's by a relative error of at most 0.0003.
Values sent between devices are 32-bit elements; how exact they have to be, the bound alone decides.
A program may use at most 128 MiB of HBM per device.

v0:
```python
import math

import jax
import jax.numpy as jnp
from jax import lax
from jax.sharding import PartitionSpec as P

ND = 36
STEPS = 2


WIND_COEF = 0.03
NONLIN_COEF = 0.004
DISS_COEF = 0.02
PLUS_WEIGHT = 0.4096
MINUS_WEIGHT = 3.1605
BOTH_WEIGHT = 1.2945
COURANT_MAX = 0.68


def padded_2(array, sides, width):
    for axis, dim in sides:
        count, length = (lax.axis_size(axis), array.shape[dim])
        up = [(i, (i + 1) % count) for i in range(count - 1)]
        down = [(j, i) for i, j in up]
        last = lax.slice_in_dim(array, length - width, length, axis=dim)
        leading = lax.slice_in_dim(array, 0, width, axis=dim)
        before = lax.ppermute(last, axis, up)
        after = lax.ppermute(leading, axis, down)
        array = jnp.concatenate([before, array, after], axis=dim)
    return array


def bin_values(bin_ids):
    frequency = (bin_ids // ND).astype(jnp.float32)
    angles = (bin_ids % ND).astype(jnp.float32) * (2.0 * math.pi / ND)
    bin_rate = 1.0 + 0.1 * frequency
    return (angles, bin_rate, 1.0 / bin_rate)


def local_sources(current, plus_hot, minus_hot, wind_speed, wind_dir, wet_point):
    bin_count = current.shape[0]
    angles, bin_rate, bin_speed = bin_values(jnp.arange(bin_count, dtype=jnp.int32))
    rounded = current.astype(jnp.bfloat16)
    plus_vals = jnp.dot(plus_hot, rounded, preferred_element_type=jnp.float32)
    minus_vals = jnp.dot(minus_hot, rounded, preferred_element_type=jnp.float32)
    delta_nl = (
        NONLIN_COEF
        * bin_rate[:, None]
        * current
        * (
            current * (PLUS_WEIGHT * plus_vals + MINUS_WEIGHT * minus_vals)
            - 2.0 * BOTH_WEIGHT * plus_vals * minus_vals
        )
    )
    delta_bf = delta_nl.astype(jnp.bfloat16)
    contract = (((0,), (0,)), ((), ()))
    returned = lax.dot_general(
        plus_hot, delta_bf, contract, preferred_element_type=jnp.float32
    ) + lax.dot_general(minus_hot, delta_bf, contract, preferred_element_type=jnp.float32)
    nonlinear = returned - 2.0 * delta_nl
    phase = 40.0 * bin_speed
    alignment = jnp.cos(angles[:, None] - wind_dir[None, :])
    growth = (
        WIND_COEF
        * bin_rate[:, None]
        * jnp.maximum(wind_speed[None, :] * alignment / phase[:, None] - 1.0, 0.0)
    )
    steepness = jnp.sqrt(jnp.mean((bin_rate[:, None] * current) ** 2, axis=0) + 1e-06)
    damping = DISS_COEF * bin_rate[:, None] * steepness[None, :]
    return wet_point[None, :] * (current + growth * current - damping * current + nonlinear)


def advect_rows(padded, first_bin, bin_span, wet_strip):
    bin_ids = first_bin + jnp.arange(bin_span, dtype=jnp.int32)
    angles, bin_rate, bin_speed = bin_values(bin_ids)
    courant_x = (COURANT_MAX * bin_speed * jnp.cos(angles))[:, None, None]
    courant_y = (COURANT_MAX * bin_speed * jnp.sin(angles))[:, None, None]
    centre = padded[:, 1:-1]
    upper_row = padded[:, :-2]
    lower_row = padded[:, 2:]
    sideways = jnp.pad(centre, ((0, 0), (0, 0), (1, 1)))
    left_cell = sideways[:, :, :-2]
    right_cell = sideways[:, :, 2:]
    advected = (
        centre
        - jnp.maximum(courant_x, 0.0) * (centre - upper_row)
        - jnp.minimum(courant_x, 0.0) * (lower_row - centre)
        - jnp.maximum(courant_y, 0.0) * (centre - left_cell)
        - jnp.minimum(courant_y, 0.0) * (right_cell - centre)
    )
    return advected * wet_strip[None]


def local(spectrum, wind_speed, wind_dir, wet_mask, row_block, plus_index, minus_index):
    bin_count = spectrum.shape[0]
    columns = spectrum.shape[1]
    wide_size = lax.axis_size("wide")
    per_dev = bin_count // wide_size
    own_index = lax.axis_index("wide")
    row_order = row_block[0]
    slot_ids = jnp.arange(wide_size, dtype=jnp.int32)
    inverse = jnp.sum(
        (row_order[None, :] == slot_ids[:, None]).astype(jnp.int32) * slot_ids[None, :], axis=1
    )
    wet_strip = wet_mask.astype(jnp.float32)
    own_row = lax.dynamic_index_in_dim(row_order, own_index, 0, keepdims=False)
    wet_point = lax.dynamic_index_in_dim(wet_strip, own_row, 0, keepdims=False)
    bin_ids = jnp.arange(bin_count, dtype=jnp.int32)
    plus_hot = (plus_index[:, None] == bin_ids[None, :]).astype(jnp.bfloat16)
    minus_hot = (minus_index[:, None] == bin_ids[None, :]).astype(jnp.bfloat16)
    current = spectrum
    for step_index in range(STEPS):
        current = local_sources(current, plus_hot, minus_hot, wind_speed, wind_dir, wet_point)
        by_device = current.reshape(wide_size, per_dev, columns)
        received = lax.all_to_all(by_device, "wide", split_axis=0, concat_axis=2, tiled=True)
        strip_grid = jnp.take(received.reshape(per_dev, wide_size, columns), inverse, axis=1)
        padded = padded_2(strip_grid, (("sub", 1),), 1)
        advected = advect_rows(padded, own_index * per_dev, per_dev, wet_strip)
        outgoing = jnp.take(advected, row_order, axis=1).reshape(1, per_dev, wide_size * columns)
        by_device = lax.all_to_all(outgoing, "wide", split_axis=2, concat_axis=0, tiled=True)
        current = by_device.reshape(bin_count, columns)
    return current


def solution(mesh):
    placed = (
        P(None, ("wide", "sub")),
        P(("wide", "sub")),
        P(("wide", "sub")),
        P("sub", None),
        P("sub", None),
        P(),
        P(),
    )
    return jax.shard_map(
        local, mesh=mesh, in_specs=placed, out_specs=P(None, ("wide", "sub")), check_vma=False
    )
```

profile of v0, /device:TPU:1, one launch (start us, length us, event | category | flops | bytes accessed | tf_op | source)
XLA Modules:
  0.0 507.7 jit_solution(3294001628954370450)
XLA Ops:
  0.0 1.3 constant_dynamic-slice_fusion
  3.6 2.1 fusion.7
  5.7 2.5 subtract_multiply_fusion.1
  8.2 1.8 fusion.2
  10.9 3.9 fusion.19
  15.8 20.4 %all-to-all-start = ((f32[128,9,128]{2,1,0:T(8,128)}), f32[128,9,128]{2,1,0:T(8,128)S(1)}, u32[]{:S(2)}, u32[]{:S(2)}) async-start(f32[128,9,128]{2,1,0:T(8,128)} %reshape.141), calls=%async_computation | async-start | bytes 2097152 | tf_op jit(solution)/shard_map/all_to_all | solution.py:116
  36.5 53.3 %all-to-all-done = f32[128,9,128]{2,1,0:T(8,128)S(1)} async-done(((f32[128,9,128]{2,1,0:T(8,128)}), f32[128,9,128]{2,1,0:T(8,128)S(1)}, u32[]{:S(2)}, u32[]{:S(2)}) %all-to-all-start) | async-done | bytes 589856 | tf_op jit(solution)/shard_map/all_to_all | solution.py:116
  90.7 9.7 %collective-permute-start = (f32[9,1,128]{2,0,1:T(8,128)S(1)}, f32[9,1,128]{2,0,1:T(8,128)S(1)}, u32[]{:S(2)}, u32[]{:S(2)}) collective-permute-start(f32[9,1,128]{2,0,1:T(8,128)S(1)} %get-tuple-element.8), channel_id=1, source_target_pairs={{0,1},{1,2},{2,3},{4,5},{5,6},{6,7},{8,9},{9,10},{10,11},{12,13},{... | collective-permute-start | bytes 13832 | tf_op jit(solution)/shard_map/ppermute | solution.py:28
  100.4 2.1 collective-permute-start.1
  102.6 11.5 %collective-permute-done.1 = f32[9,1,128]{2,0,1:T(8,128)S(1)} collective-permute-done((f32[9,1,128]{2,0,1:T(8,128)S(1)}, f32[9,1,128]{2,0,1:T(8,128)S(1)}, u32[]{:S(2)}, u32[]{:S(2)}) %collective-permute-start.1) | collective-permute-done | bytes 4640 | tf_op jit(solution)/shard_map/ppermute | solution.py:29
  115.8 4.7 copy.28
  120.9 74.4 %reduce.1 = f32[16384,9]{1,0:T(8,128)} reduce(f32[16384,1,9]{2,1,0:T(1,128)} %bitcast.41, f32[]{:T(128)} %broadcast.640), dimensions={1}, to_apply=%bitcast.37.reduce_sub_computation | reduce | bytes 1179652
  195.3 8.7 %reshape.193 = f32[128,1,1152]{2,1,0:T(1,128)} reshape(f32[16384,9]{1,0:T(8,128)} %reduce.1) | data formatting | bytes 1179648
  204.0 7.8 %all-to-all-start.1 = ((f32[128,1,1152]{2,1,0:T(1,128)}), f32[128,1,1152]{2,1,0:T(1,128)S(1)}, u32[]{:S(2)}, u32[]{:S(2)}) async-start(f32[128,1,1152]{2,1,0:T(1,128)} %reshape.193), calls=%async_computation.1 | async-start | bytes 1179648 | tf_op jit(solution)/shard_map/all_to_all | solution.py:121
  211.8 25.1 %all-to-all-done.1 = f32[128,1,1152]{2,1,0:T(1,128)S(1)} async-done(((f32[128,1,1152]{2,1,0:T(1,128)}), f32[128,1,1152]{2,1,0:T(1,128)S(1)}, u32[]{:S(2)}, u32[]{:S(2)}) %all-to-all-start.1) | async-done | bytes 589856 | tf_op jit(solution)/shard_map/all_to_all | solution.py:121
  236.9 2.0 reduce.2
  238.9 14.1 %reshape.194 = f32[16384,1,9]{2,1,0:T(1,128)} reshape(f32[128,1152]{1,0:T(8,128)S(1)} %reduce.2) | data formatting | bytes 1179648
  252.9 15.2 %copy.22 = f32[1,9,16384]{2,0,1:T(1,128)S(1)} copy(f32[1,9,16384]{1,0,2:T(1,128)} %bitcast.43) | data formatting | bytes 1179648 | tf_op jit(solution)/shard_map/all_to_all | solution.py:121
  269.7 1.1 subtract_multiply_fusion
  270.8 1.7 fusion
  272.8 3.9 fusion.23
  276.8 59.7 %all_to_all.60 = f32[128,9,128]{2,1,0:T(8,128)S(1)} all-to-all(f32[128,9,128]{2,1,0:T(8,128)S(1)} %reshape.145), channel_id=1, replica_groups=mesh['wide'=128,'sub'=4] {'wide'}, dimensions={0} | all-to-all | bytes 1179648 | tf_op jit(solution)/shard_map/all_to_all | solution.py:116
  337.4 1.9 collective-permute-start.2
  339.3 2.8 collective-permute-start.3
  342.2 10.9 %collective-permute-done.3 = f32[9,1,128]{2,0,1:T(8,128)S(1)} collective-permute-done((f32[9,1,128]{2,0,1:T(8,128)S(1)}, f32[9,1,128]{2,0,1:T(8,128)S(1)}, u32[]{:S(2)}, u32[]{:S(2)}) %collective-permute-start.3) | collective-permute-done | bytes 4640 | tf_op jit(solution)/shard_map/ppermute | solution.py:29
  354.7 4.7 copy.29
  359.4 74.4 %reduce.3 = f32[16384,9]{1,0:T(8,128)} reduce(f32[16384,1,9]{2,1,0:T(1,128)} %bitcast.42, f32[]{:T(128)} %broadcast.640), dimensions={1}, to_apply=%bitcast.39.reduce_sub_computation | reduce | bytes 1179652
  433.7 8.0 %reshape.195 = f32[128,1,1152]{2,1,0:T(1,128)S(1)} reshape(f32[16384,9]{1,0:T(8,128)} %reduce.3) | data formatting | bytes 1179648
  441.7 33.5 %all_to_all.61 = f32[128,1,1152]{2,1,0:T(1,128)S(1)} all-to-all(f32[128,1,1152]{2,1,0:T(1,128)S(1)} %reshape.195), channel_id=1, replica_groups=mesh['wide'=128,'sub'=4] {'wide'}, dimensions={0} | all-to-all | bytes 1179648 | tf_op jit(solution)/shard_map/all_to_all | solution.py:121
  475.2 2.0 reduce.4
  477.2 14.1 %reshape.196 = f32[16384,1,9]{2,1,0:T(1,128)} reshape(f32[128,1152]{1,0:T(8,128)S(1)} %reduce.4) | data formatting | bytes 1179648
  491.2 15.0 %copy.26 = f32[1,9,16384]{2,0,1:T(1,128)S(1)} copy(f32[1,9,16384]{1,0,2:T(1,128)} %bitcast.44) | data formatting | bytes 1179648 | tf_op jit(solution)/shard_map/all_to_all | solution.py:121
  (54 shorter events, 11.3 us)
Async XLA Ops:
  0.0 10.9 %copy-start.2 = (s32[1152]{0:T(1024)S(1)}, s32[1152]{0:T(1024)}, u32[]{:S(2)}) copy-start(s32[1152]{0:T(1024)} %param.14) | copy-start | bytes 13828
  0.0 9.9 %copy-start = (f32[1152,128]{1,0:T(8,128)S(1)}, f32[1152,128]{1,0:T(8,128)}, u32[]{:S(2)}) copy-start(f32[1152,128]{1,0:T(8,128)} %param.9) | copy-start | bytes 1769476
  0.0 8.2 %copy-start.1 = (s32[1152]{0:T(1024)S(1)}, s32[1152]{0:T(1024)}, u32[]{:S(2)}) copy-start(s32[1152]{0:T(1024)} %param.15) | copy-start | bytes 13828
  0.0 10.9 %copy-start.5 = (f32[128]{0:T(128)S(1)}, f32[128]{0:T(128)}, u32[]{:S(2)}) copy-start(f32[128]{0:T(128)} %param.10) | copy-start | bytes 1540
  0.0 10.9 %copy-start.4 = (f32[128]{0:T(128)S(1)}, f32[128]{0:T(128)}, u32[]{:S(2)}) copy-start(f32[128]{0:T(128)} %param.11) | copy-start | bytes 1540
  10.2 26.1 %copy-start.3 = (s32[1,128]{1,0:T(1,128)S(1)}, s32[1,128]{1,0:T(1,128)}, u32[]{:S(2)}) copy-start(s32[1,128]{1,0:T(1,128)} %param.13) | copy-start | bytes 1540
  15.8 73.9 %all-to-all-start = ((f32[128,9,128]{2,1,0:T(8,128)}), f32[128,9,128]{2,1,0:T(8,128)S(1)}, u32[]{:S(2)}, u32[]{:S(2)}) async-start(f32[128,9,128]{2,1,0:T(8,128)} %reshape.141), calls=%async_computation | async-start | bytes 2097152 | tf_op jit(solution)/shard_map/all_to_all | solution.py:116
  90.7 11.8 %collective-permute-start = (f32[9,1,128]{2,0,1:T(8,128)S(1)}, f32[9,1,128]{2,0,1:T(8,128)S(1)}, u32[]{:S(2)}, u32[]{:S(2)}) collective-permute-start(f32[9,1,128]{2,0,1:T(8,128)S(1)} %get-tuple-element.8), channel_id=1, source_target_pairs={{0,1},{1,2},{2,3},{4,5},{5,6},{6,7},{8,9},{9,10},{10,11},{12,13},{... | collective-permute-start | bytes 13832 | tf_op jit(solution)/shard_map/ppermute | solution.py:28
  100.4 13.7 %collective-permute-start.1 = (f32[9,1,128]{2,0,1:T(8,128)S(1)}, f32[9,1,128]{2,0,1:T(8,128)S(1)}, u32[]{:S(2)}, u32[]{:S(2)}) collective-permute-start(f32[9,1,128]{2,0,1:T(8,128)S(1)} %get-tuple-element.9), channel_id=1, source_target_pairs={{1,0},{2,1},{3,2},{5,4},{6,5},{7,6},{9,8},{10,9},{11,10},{13,12},{... | collective-permute-start | bytes 13832 | tf_op jit(solution)/shard_map/ppermute | solution.py:29
  204.0 33.0 %all-to-all-start.1 = ((f32[128,1,1152]{2,1,0:T(1,128)}), f32[128,1,1152]{2,1,0:T(1,128)S(1)}, u32[]{:S(2)}, u32[]{:S(2)}) async-start(f32[128,1,1152]{2,1,0:T(1,128)} %reshape.193), calls=%async_computation.1 | async-start | bytes 1179648 | tf_op jit(solution)/shard_map/all_to_all | solution.py:121
  337.4 4.7 collective-permute-start.2
  339.3 13.7 %collective-permute-start.3 = (f32[9,1,128]{2,0,1:T(8,128)S(1)}, f32[9,1,128]{2,0,1:T(8,128)S(1)}, u32[]{:S(2)}, u32[]{:S(2)}) collective-permute-start(f32[9,1,128]{2,0,1:T(8,128)S(1)} %get-tuple-element.7), channel_id=1, source_target_pairs={{1,0},{2,1},{3,2},{5,4},{6,5},{7,6},{9,8},{10,9},{11,10},{13,12},{... | collective-permute-start | bytes 13832 | tf_op jit(solution)/shard_map/ppermute | solution.py:29
where the time goes:
time: 517 us; the launch traced here: 508 us
  other arithmetic  157 us (30%)
  waiting for transfers between devices  101 us (20%)
  blocking collectives  93.1 us (18%)
  local copies, waits for them, and re-layouts  92 us (18%)
  starting transfers between devices  44.7 us (9%)
  matrix products  18 us (3%)
    unnamed x2, other arithmetic  149 us
    all_to_all x1, blocking collectives, local(): lax.all_to_all(by_device, 'wide', split_axis=0, concat_axis=2, tiled=True)  59.7 us
    all_to_all x1, waiting for transfers between devices, local(): lax.all_to_all(by_device, 'wide', split_axis=0, concat_axis=2, tiled=True)  53.3 us
    unnamed x17, local copies, waits for them, and re-layouts  45.3 us
    all_to_all x1, blocking collectives, local(): lax.all_to_all(outgoing, 'wide', split_axis=2, concat_axis=0, tiled=True)  33.5 us
    all_to_all x4, local copies, waits for them, and re-layouts, local(): lax.all_to_all(outgoing, 'wide', split_axis=2, concat_axis=0, tiled=True)  30.9 us
    all_to_all x1, waiting for transfers between devices, local(): lax.all_to_all(outgoing, 'wide', split_axis=2, concat_axis=0, tiled=True)  25.1 us
    ppermute x2, waiting for transfers between devices, padded_2(): after = lax.ppermute(leading, axis, down)  22.4 us
  transfers between devices with their start and end apart: 6, of which 4 were waited for; matrix products, arithmetic and copies ran while one was open for 0% of the time, Pallas kernels for 0%

commit v1 on v0

v1 whole, which is shorter than its diff:
```python
import functools
import math

import jax
import jax.numpy as jnp
import numpy as np
from jax import lax
from jax.experimental import pallas as pl
from jax.experimental.pallas import tpu as pltpu
from jax.sharding import PartitionSpec as P

ND = 36
NF = 32
NB = ND * NF
NW = 128
NS = 4
TILES = NB // 128
HALF = 5 * 128
SPLIT = 19 * NF

WIND_COEF = 0.03
NONLIN_COEF = 0.004
DISS_COEF = 0.02
PLUS_WEIGHT = 0.4096
MINUS_WEIGHT = 3.1605
BOTH_WEIGHT = 1.2945
COURANT_MAX = 0.68
MESH = pl.DeviceIdType.MESH
F32 = jnp.float32
BF16 = jnp.bfloat16

RATE, GROW_X, GROW_Y, GROW_0, DAMP, DELTA, KEEP, MOVE_X, MOVE_Y, EAST = range(10)


def bin_table():
    new = np.arange(NB)
    k, l = (new % NF).astype(np.float32), (new // NF).astype(np.float32)
    angles = l * np.float32(2.0 * math.pi / ND)
    rate = np.float32(1.0) + np.float32(0.1) * k
    speed = np.float32(1.0) / rate
    cx = np.float32(COURANT_MAX) * speed * np.cos(angles)
    cy = np.float32(COURANT_MAX) * speed * np.sin(angles)
    table = np.zeros((16, NB), np.float32)
    table[RATE] = rate
    table[GROW_X] = WIND_COEF * rate * rate / 40.0 * np.cos(angles)
    table[GROW_Y] = WIND_COEF * rate * rate / 40.0 * np.sin(angles)
    table[GROW_0] = WIND_COEF * rate
    table[DAMP] = DISS_COEF * rate
    table[DELTA] = NONLIN_COEF * rate
    table[KEEP] = 1.0 - np.abs(cx) - np.abs(cy)
    table[MOVE_X] = np.abs(cx)
    table[MOVE_Y] = np.abs(cy)
    table[EAST] = cx > 0
    assert (cy[:SPLIT] >= 0).all() and (cy[SPLIT:] <= 0).all()
    return table


def column_of(w):
    plane, z = w // 8, lax.rem(w, 8)
    y, x = plane // 4, lax.rem(plane, 4)
    turn = lax.rem(y, 2)
    p = y * 4 + x + turn * (3 - 2 * x)
    back = lax.rem(z, 2)
    return z * 16 + p + back * (15 - 2 * p)


def device_of(c):
    z, q = c // 16, lax.rem(c, 16)
    back = lax.rem(z, 2)
    p = q + back * (15 - 2 * q)
    y, i = p // 4, lax.rem(p, 4)
    turn = lax.rem(y, 2)
    x = i + turn * (3 - 2 * i)
    return (y * 4 + x) * 8 + z


def lanes(t, count=1):
    return pl.ds(pl.multiple_of(t * 128, 128), 128 * count)


def build_partners(part_ref, hot_ref):
    rows = lax.broadcasted_iota(jnp.int32, (256, 256), 0)

    def one(t, carry):
        hot_ref[t] = (part_ref[t] == rows).astype(F32).astype(BF16)
        return carry

    lax.fori_loop(0, TILES, one, 0)


def sources(field, wind_x, wind_y, wet, tab_ref, hot_ref, round_ref, pair_ref, delta_ref, add_ref):
    def rounding(t, total):
        f = field[:, lanes(t)]
        round_ref[:, lanes(t)] = f.astype(BF16)
        scaled = f * tab_ref[RATE : RATE + 1, lanes(t)]
        return total + scaled * scaled

    total = lax.fori_loop(0, TILES, rounding, jnp.zeros((128, 128), F32))
    round_ref[:, lanes(TILES)] = round_ref[:, lanes(0)]
    steep = jnp.sqrt(jnp.sum(total, axis=1, keepdims=True) * (1.0 / NB) + 1e-06)
    steep = jnp.broadcast_to(steep, (128, 128))

    def gather(t, carry):
        both = jnp.dot(round_ref[:, lanes(t, 2)], hot_ref[t], preferred_element_type=F32)
        pair_ref[0, :, lanes(t)] = both[:, :128]
        pair_ref[1, :, lanes(lax.rem(t + 1, TILES))] = both[:, 128:]
        return carry

    lax.fori_loop(0, TILES, gather, 0)

    def combine(t, carry):
        f = field[:, lanes(t)]
        plus, minus = pair_ref[0, :, lanes(t)], pair_ref[1, :, lanes(t)]
        row = lambda r: tab_ref[r : r + 1, lanes(t)]
        delta = (row(DELTA) * f) * (
            f * (PLUS_WEIGHT * plus + MINUS_WEIGHT * minus) - (2.0 * BOTH_WEIGHT) * plus * minus
        )
        delta_ref[:, lanes(t)] = delta.astype(BF16)
        growth = jnp.maximum(wind_x * row(GROW_X) + wind_y * row(GROW_Y) - row(GROW_0), 0.0)
        field[:, lanes(t)] = f + growth * f - (row(DAMP) * steep) * f - 2.0 * delta
        return carry

    lax.fori_loop(0, TILES, combine, 0)
    delta_ref[:, lanes(TILES)] = delta_ref[:, lanes(0)]

    def scatter(t, carry):
        back = lax.dot_general(
            delta_ref[:, lanes(t, 2)], hot_ref[t], (((1,), (1,)), ((), ())), preferred_element_type=F32
        )
        add_ref[0, :, lanes(t)] = back[:, :128]
        add_ref[1, :, lanes(lax.rem(t + 1, TILES))] = back[:, 128:]
        return carry

    lax.fori_loop(0, TILES, scatter, 0)

    def finish(t, carry):
        field[:, lanes(t)] = wet * (field[:, lanes(t)] + add_ref[0, :, lanes(t)] + add_ref[1, :, lanes(t)])
        return carry

    lax.fori_loop(0, TILES, finish, 0)


def spread(row):
    return jnp.transpose(jnp.broadcast_to(row, (128, 128)))


def advect(src, dst, west, east, edges, shift, rows, wet, tab_ref):
    lane = lax.broadcasted_iota(jnp.int32, (128, 128), 1)
    top, bottom = rows == 0.0, rows == float(NW - 1)
    for t in range(TILES):
        at = slice(t * 128, t * 128 + 128)
        f = src[:, at]
        high = f.astype(BF16)
        low = (f - high.astype(F32)).astype(BF16)
        moved = jnp.dot(shift, jnp.concatenate([high, low], axis=0), preferred_element_type=F32)
        above = jnp.where(top, edges[0:1, at], moved[:128])
        below = jnp.where(bottom, edges[8:9, at], moved[128:])
        row = lambda r: tab_ref[r : r + 1, at]
        near_x = jnp.where(row(EAST) > 0.5, above, below)
        if t < 4:
            near_y = west[:, at]
        elif t > 4:
            near_y = east[:, (t - 4) * 128 : (t - 3) * 128]
        else:
            near_y = jnp.where(lane < SPLIT - 512, west[:, at], east[:, 0:128])
        dst[:, at] = wet * (row(KEEP) * f + row(MOVE_X) * near_x + row(MOVE_Y) * near_y)


def kernel(
    spectrum,
    speed,
    direction,
    wet_ref,
    order_ref,
    part_ref,
    tab_ref,
    out,
    first,
    second,
    last,
    wind_out,
    wind_in,
    west,
    east,
    edge_out,
    edge_in,
    hot,
    rounded,
    pair,
    delta,
    add,
    send_a,
    recv_a,
    send_w,
    recv_w,
    send_h,
    recv_h,
    send_e,
    recv_e,
    send_b,
    recv_b,
    spare,
    spare_w,
):
    me = lax.axis_index("wide")
    strip = lax.axis_index("sub")
    column = column_of(me)
    lower, upper = column > 0, column < NW - 1
    to_lower, to_upper = device_of(jnp.maximum(column - 1, 0)), device_of(jnp.minimum(column + 1, NW - 1))
    has_above, has_below = strip > 0, strip < NS - 1

    for k in range(2):
        for is_there, blank in (
            (lower, west.at[k]),
            (upper, east.at[k]),
            (has_above, edge_in.at[k, 0:8]),
            (has_below, edge_in.at[k, 8:16]),
        ):

            @pl.when(jnp.logical_not(is_there))
            def _(blank=blank):
                blank[...] = jnp.zeros(blank.shape, F32)

    barrier = pltpu.get_barrier_semaphore()

    def greet(i, carry):
        pl.semaphore_signal(
            barrier, inc=1, device_id={"wide": lax.rem(me + i, NW)}, device_id_type=MESH
        )
        return carry

    lax.fori_loop(1, NW, greet, 0)

    @pl.when(has_above)
    def _():
        pl.semaphore_signal(barrier, inc=1, device_id={"sub": strip - 1}, device_id_type=MESH)

    @pl.when(has_below)
    def _():
        pl.semaphore_signal(barrier, inc=1, device_id={"sub": strip + 1}, device_id_type=MESH)

    row_ids = lax.broadcasted_iota(jnp.int32, (128, 128), 0).astype(F32)
    lane_ids = lax.broadcasted_iota(jnp.int32, (128, 128), 1).astype(F32)
    ones = jnp.ones((128, 128), BF16)
    order = order_ref[...].astype(F32)
    rows = spread(order)
    wet_grid = wet_ref[...].astype(F32)
    mine = jnp.sum(jnp.where(lane_ids == me.astype(F32), order, 0.0), axis=1, keepdims=True)
    own_wet = jnp.where(row_ids == mine, wet_grid, 0.0).astype(BF16)
    own_wet = lax.dot_general(own_wet, ones, (((0,), (0,)), ((), ())), preferred_element_type=F32)
    col_wet = jnp.where(lane_ids == column.astype(F32), wet_grid, 0.0).astype(BF16)
    col_wet = jnp.dot(col_wet, ones, preferred_element_type=F32).astype(BF16)
    pick = (lane_ids == rows).astype(F32).astype(BF16)
    col_wet = jnp.dot(pick, col_wet, preferred_element_type=F32)
    above_hot = (order == rows - 1.0).astype(F32)
    below_hot = (order == rows + 1.0).astype(F32)
    shift = jnp.concatenate([above_hot, below_hot], axis=0)
    shift = jnp.concatenate([shift, shift], axis=1).astype(BF16)

    wind_x = spread(speed[...] * jnp.cos(direction[...]))
    wind_y = spread(speed[...] * jnp.sin(direction[...]))
    wind_out[...] = jnp.where(lane_ids < 64.0, wind_x, wind_y)

    build_partners(part_ref, hot)
    for t in range(TILES):
        block = jnp.concatenate([spectrum[pl.ds(4 * t + i, NF, stride=ND), :] for i in range(4)], axis=0)
        first[:, t * 128 : t * 128 + 128] = jnp.transpose(block)
    sources(first, wind_x, wind_y, own_wet, tab_ref, hot, rounded, pair, delta, add)

    pl.semaphore_wait(barrier, NW - 1 + has_above.astype(jnp.int32) + has_below.astype(jnp.int32))

    one = lambda ref, i: ref.at[pl.ds(i, 1)]
    pltpu.make_async_copy(one(first, column), one(second, me), recv_a).start()
    pltpu.make_async_copy(one(first, column), one(spare, 0), send_a).start()
    pltpu.make_async_copy(one(wind_out, column), one(wind_in, me), recv_w).start()
    pltpu.make_async_copy(one(wind_out, column), one(spare_w, 0), send_w).start()

    def send_out(i, carry):
        w = lax.rem(me + i, NW)
        c = column_of(w)
        for src, dst, s, r in ((wind_out, wind_in, send_w, recv_w), (first, second, send_a, recv_a)):
            pltpu.make_async_remote_copy(
                one(src, c), one(dst, me), s, r, device_id={"wide": w}, device_id_type=MESH
            ).start()
        return carry

    lax.fori_loop(1, NW, send_out, 0)

    def wait_rows(ref, sem):
        pltpu.make_async_copy(ref, ref, sem).wait()

    def halo(k, field):
        total_top = jnp.zeros((1, 128), F32)
        for t in range(TILES):
            at = slice(t * 128, t * 128 + 128)
            f = field[:, at]
            edge_out[k, 0:1, at] = jnp.sum(jnp.where(rows == float(NW - 1), f, 0.0), axis=0, keepdims=True)
            edge_out[k, 8:9, at] = jnp.sum(jnp.where(rows == 0.0, f, 0.0), axis=0, keepdims=True)
        copies = (
            (upper, lower, field.at[:, 0:HALF], west.at[k], {"wide": to_upper}, send_h.at[k, 0], recv_h.at[k, 0]),
            (lower, upper, field.at[:, NB - HALF : NB], east.at[k], {"wide": to_lower}, send_h.at[k, 1], recv_h.at[k, 1]),
            (
                has_below,
                has_above,
                edge_out.at[k, 0:8],
                edge_in.at[k, 0:8],
                {"sub": jnp.minimum(strip + 1, NS - 1)},
                send_e.at[k, 0],
                recv_e.at[k, 0],
            ),
            (
                has_above,
                has_below,
                edge_out.at[k, 8:16],
                edge_in.at[k, 8:16],
                {"sub": jnp.maximum(strip - 1, 0)},
                send_e.at[k, 1],
                recv_e.at[k, 1],
            ),
        )
        for sends, gets, src, dst, to, s, r in copies:
            copy = pltpu.make_async_remote_copy(src, dst, s, r, device_id=to, device_id_type=MESH)
            pl.when(sends)(copy.start)
        for sends, gets, src, dst, to, s, r in copies:
            copy = pltpu.make_async_remote_copy(src, dst, s, r, device_id=to, device_id_type=MESH)
            pl.when(gets)(copy.wait_recv)
            pl.when(sends)(copy.wait_send)

    wait_rows(second, recv_a)
    halo(0, second)
    wait_rows(first, send_a)
    advect(second, first, west.at[0], east.at[0], edge_in.at[0], shift, rows, col_wet, tab_ref)

    wait_rows(wind_in, recv_w)
    both = wind_in[...]
    turned = pltpu.roll(both, 64, 1)
    wind_x = jnp.where(lane_ids < 64.0, both, turned)
    wind_y = jnp.where(lane_ids < 64.0, turned, both)
    sources(first, wind_x, wind_y, col_wet, tab_ref, hot, rounded, pair, delta, add)
    halo(1, first)
    advect(first, second, west.at[1], east.at[1], edge_in.at[1], shift, rows, col_wet, tab_ref)

    pltpu.make_async_copy(one(second, me), one(last, column), recv_b).start()
    pltpu.make_async_copy(one(second, me), one(spare, 8), send_b).start()

    def send_back(i, carry):
        w = lax.rem(me + i, NW)
        pltpu.make_async_remote_copy(
            one(second, w), one(last, column), send_b, recv_b, device_id={"wide": w}, device_id_type=MESH
        ).start()
        return carry

    lax.fori_loop(1, NW, send_back, 0)
    wait_rows(last, recv_b)
    for t in range(TILES):
        block = jnp.transpose(last[:, t * 128 : t * 128 + 128])
        for i in range(4):
            out[pl.ds(4 * t + i, NF, stride=ND), :] = block[i * NF : (i + 1) * NF]
    wait_rows(wind_out, send_w)
    wait_rows(second, send_b)


def local(spectrum, wind_speed, wind_dir, wet_mask, row_block, plus_index, minus_index):
    new = np.arange(NB)
    old = jnp.asarray((new % NF) * ND + new // NF)
    turned = lambda index: lax.rem(index, ND) * NF + lax.div(index, ND)
    up, down = turned(plus_index)[old], turned(minus_index)[old]
    up = up.reshape(TILES, 1, 128)
    down = jnp.roll(down.reshape(TILES, 1, 128), -1, axis=0)
    base = jnp.arange(TILES, dtype=jnp.int32).reshape(TILES, 1, 1) * 128
    part = lax.rem(jnp.concatenate([up, down], axis=2) - base + NB, NB)
    dma, f32 = pltpu.SemaphoreType.DMA, F32
    vmem = pl.BlockSpec(memory_space=pltpu.VMEM)
    wide = NB + 128
    return pl.pallas_call(
        kernel,
        out_shape=jax.ShapeDtypeStruct((NB, 128), f32),
        in_specs=[vmem] * 7,
        out_specs=vmem,
        scratch_shapes=[
            pltpu.VMEM((128, NB), f32),
            pltpu.VMEM((128, NB), f32),
            pltpu.VMEM((128, NB), f32),
            pltpu.VMEM((128, 128), f32),
            pltpu.VMEM((128, 128), f32),
            pltpu.VMEM((2, 128, HALF), f32),
            pltpu.VMEM((2, 128, HALF), f32),
            pltpu.VMEM((2, 16, NB), f32),
            pltpu.VMEM((2, 16, NB), f32),
            pltpu.VMEM((TILES, 256, 256), BF16),
            pltpu.VMEM((128, wide), BF16),
            pltpu.VMEM((2, 128, NB), f32),
            pltpu.VMEM((128, wide), BF16),
            pltpu.VMEM((2, 128, NB), f32),
            dma,
            dma,
            dma,
            dma,
            dma((2, 2)),
            dma((2, 2)),
            dma((2, 2)),
            dma((2, 2)),
            dma,
            dma,
            pltpu.VMEM((16, NB), f32),
            pltpu.VMEM((8, 128), f32),
        ],
        compiler_params=pltpu.CompilerParams(
            collective_id=0, has_side_effects=True, vmem_limit_bytes=48 * 2**20
        ),
    )(
        spectrum,
        wind_speed.reshape(1, 128),
        wind_dir.reshape(1, 128),
        wet_mask,
        row_block,
        part,
        jnp.asarray(bin_table()),
    )


def solution(mesh):
    placed = (
        P(None, ("wide", "sub")),
        P(("wide", "sub")),
        P(("wide", "sub")),
        P("sub", None),
        P("sub", None),
        P(),
        P(),
    )
    return jax.shard_map(
        local, mesh=mesh, in_specs=placed, out_specs=P(None, ("wide", "sub")), check_vma=False
    )
```

time: 517 us -> 120 us (0.23); the launches traced: 508 us -> 120 us
  other arithmetic: 157 us -> 0.84 us
  Pallas kernels: 0 us -> 104 us
  waiting for transfers between devices: 101 us -> 0 us
  blocking collectives: 93.1 us -> 0 us
  local copies, waits for them, and re-layouts: 92 us -> 15 us
  starting transfers between devices: 44.7 us -> 0 us
  matrix products: 18 us -> 0 us
    unnamed x2 -> x0, other arithmetic: 149 us -> none
    pallas_call x0 -> x1, Pallas kernels: none -> 104 us  [local(): pl.pallas_call(kernel, out_shape=jax.ShapeDtypeStruct((NB, 128), f32), in...]
    all_to_all x2 -> x0, blocking collectives: 93.1 us -> none  [the longest x1 59.7 us: local(): lax.all_to_all(by_device, 'wide', split_axis=0, concat_axis=2, tiled=True)]
    all_to_all x2 -> x0, waiting for transfers between devices: 78.4 us -> none  [the longest x1 53.3 us: local(): lax.all_to_all(by_device, 'wide', split_axis=0, concat_axis=2, tiled=True)]
    unnamed x17, local copies, waits for them, and re-layouts: 45.3 us -> 2.04 us
    all_to_all x4 -> x0, local copies, waits for them, and re-layouts: 30.9 us -> none  [local(): lax.all_to_all(outgoing, 'wide', split_axis=2, concat_axis=0, tiled=True)]
    all_to_all x2 -> x0, starting transfers between devices: 28.2 us -> none  [the longest x1 20.4 us: local(): lax.all_to_all(by_device, 'wide', split_axis=0, concat_axis=2, tiled=True)]
    ppermute x4 -> x0, waiting for transfers between devices: 22.4 us -> none  [the longest x2 22.4 us: padded_2(): after = lax.ppermute(leading, axis, down)]
  transfers between devices with their start and end apart: 6 -> 0, of which waited for: 4 -> 0; matrix products, arithmetic and copies ran while one was open for 0% -> 0% of each run, Pallas kernels for 0% -> 0%
where the time goes in v1:
time: 120 us
  Pallas kernels  104 us (87%)
  local copies, waits for them, and re-layouts  15 us (12%)
    pallas_call x1, Pallas kernels, local(): pl.pallas_call(kernel, out_shape=jax.ShapeDtypeStruct((NB, 128), f32), in...  104 us
    gather x2, local copies, waits for them, and re-layouts, local(): up, down = (turned(plus_index)[old], turned(minus_index)[old])  13 us

profile of v1, /device:TPU:1, one launch (start us, length us, event | category | flops | bytes accessed | tf_op | source)
XLA Modules:
  0.0 120.0 jit_solution(15499547434853949116)
XLA Ops:
  0.0 0.0 copy-start.6
  0.0 0.7 pad_clamp_fusion
  0.7 0.0 copy-done.6
  0.7 6.5 %gather_fusion = s32[1152]{0:T(1024)S(1)} fusion(s32[1152]{0:T(1024)S(1)} %divide_add_fusion.1, s32[2048]{0:T(1024)S(1)} %pad_clamp_fusion), kind=kCustom, calls=%fused_computation | custom fusion | bytes 13824 | tf_op jit(solution)/shard_map/gather | solution.py:367
  7.2 0.0 copy-start.7
  7.2 0.7 copy-done.7
  7.9 0.0 copy-start
  7.9 0.0 copy-start.1
  7.9 0.0 copy-start.2
  8.0 6.5 %gather_fusion.1 = s32[1152]{0:T(1024)S(1)} fusion(s32[1152]{0:T(1024)S(1)} %divide_add_fusion, s32[2048]{0:T(1024)S(1)} %pad_clamp_fusion), kind=kCustom, calls=%fused_computation.1 | custom fusion | bytes 13824 | tf_op jit(solution)/shard_map/gather | solution.py:367
  14.5 0.0 copy-start.3
  14.5 0.0 copy-start.4
  14.5 0.0 copy-start.5
  14.5 0.1 fusion.1.part_ref
  14.6 0.0 copy-done
  14.6 0.0 copy-done.1
  14.6 0.0 copy-done.2
  14.6 0.5 copy-done.3
  15.1 0.0 copy-done.4
  15.1 0.0 copy-done.5
  15.2 104.0 %shard_map.91 = f32[1152,128]{1,0:T(8,128)S(1)} custom-call(f32[1152,128]{1,0:T(8,128)S(1)} %copy-done, f32[1,128]{1,0:T(1,128)S(1)} %bitcast.5, f32[1,128]{1,0:T(1,128)S(1)} %bitcast.6, s32[128,128]{1,0:T(8,128)S(1)} %copy-done.2, s32[1,128]{1,0:T(1,128)S(1)} %copy-done.5, s32[9,1,256]{2,1,0:T(1,128)S(1)} %fusion.1.part_ref, f32[16,1152]{1,0:T(8,128)S(1)} %copy-done.1), custom_call_target="tpu_custom_call" | custom-call | tf_op jit(solution)/shard_map/pallas_call | solution.py:375
  119.1 0.8 copy.11
  (6 shorter events, 0.0 us)
Async XLA Ops:
  0.0 0.7 copy-start.6
  7.2 0.7 copy-start.7
  7.9 6.7 %copy-start = (f32[1152,128]{1,0:T(8,128)S(1)}, f32[1152,128]{1,0:T(8,128)}, u32[]{:S(2)}) copy-start(f32[1152,128]{1,0:T(8,128)} %spectrum.1) | copy-start | bytes 1769476
  7.9 6.7 %copy-start.1 = (f32[16,1152]{1,0:T(8,128)S(1)}, f32[16,1152]{1,0:T(8,128)}, u32[]{:S(2)}) copy-start(f32[16,1152]{1,0:T(8,128)} %constant.16.clone.tab_ref) | copy-start | bytes 221188
  7.9 6.7 %copy-start.2 = (s32[128,128]{1,0:T(8,128)S(1)}, s32[128,128]{1,0:T(8,128)}, u32[]{:S(2)}) copy-start(s32[128,128]{1,0:T(8,128)} %wet_ref.1) | copy-start | bytes 196612
  14.5 0.7 copy-start.3
  14.5 0.7 copy-start.4
  14.5 0.7 copy-start.5

commit v2 on v1

v2 whole, which is shorter than its diff:
```python
import functools
import math

import jax
import jax.numpy as jnp
import numpy as np
from jax import lax
from jax.experimental import pallas as pl
from jax.experimental.pallas import tpu as pltpu
from jax.sharding import PartitionSpec as P

ND = 36
NF = 32
NB = ND * NF
NW = 128
NS = 4
TILES = NB // 128
HALF = 5 * 128
SPLIT = 19 * NF

WIND_COEF = 0.03
NONLIN_COEF = 0.004
DISS_COEF = 0.02
PLUS_WEIGHT = 0.4096
MINUS_WEIGHT = 3.1605
BOTH_WEIGHT = 1.2945
COURANT_MAX = 0.68
MESH = pl.DeviceIdType.MESH
F32 = jnp.float32
BF16 = jnp.bfloat16

RATE, GROW_X, GROW_Y, GROW_0, DAMP, DELTA, KEEP, MOVE_UP, MOVE_DOWN, MOVE_Y = range(10)


def bin_table():
    new = np.arange(NB)
    k, l = (new % NF).astype(np.float32), (new // NF).astype(np.float32)
    angles = l * np.float32(2.0 * math.pi / ND)
    rate = np.float32(1.0) + np.float32(0.1) * k
    speed = np.float32(1.0) / rate
    cx = np.float32(COURANT_MAX) * speed * np.cos(angles)
    cy = np.float32(COURANT_MAX) * speed * np.sin(angles)
    table = np.zeros((16, NB), np.float32)
    table[RATE] = rate
    table[GROW_X] = WIND_COEF * rate * rate / 40.0 * np.cos(angles)
    table[GROW_Y] = WIND_COEF * rate * rate / 40.0 * np.sin(angles)
    table[GROW_0] = WIND_COEF * rate
    table[DAMP] = DISS_COEF * rate
    table[DELTA] = NONLIN_COEF * rate
    table[KEEP] = 1.0 - np.abs(cx) - np.abs(cy)
    table[MOVE_UP] = np.maximum(cx, 0.0)
    table[MOVE_DOWN] = np.maximum(-cx, 0.0)
    table[MOVE_Y] = np.abs(cy)
    assert (cy[:SPLIT] >= 0).all() and (cy[SPLIT:] <= 0).all()
    return table


def column_of(w):
    plane, z = w // 8, lax.rem(w, 8)
    y, x = plane // 4, lax.rem(plane, 4)
    turn = lax.rem(y, 2)
    p = y * 4 + x + turn * (3 - 2 * x)
    back = lax.rem(z, 2)
    return z * 16 + p + back * (15 - 2 * p)


def device_of(c):
    z, q = c // 16, lax.rem(c, 16)
    back = lax.rem(z, 2)
    p = q + back * (15 - 2 * q)
    y, i = p // 4, lax.rem(p, 4)
    turn = lax.rem(y, 2)
    x = i + turn * (3 - 2 * i)
    return (y * 4 + x) * 8 + z


def lanes(t, count=1):
    start = t * 128 if isinstance(t, int) else pl.multiple_of(t * 128, 128)
    return pl.ds(start, 128 * count)


def chunk(g, size=32):
    return pl.ds(pl.multiple_of(g * size, size), size)


def spread(row):
    return jnp.transpose(jnp.broadcast_to(row, (128, 128)))


def build_partners(up_ref, down_ref, column_ref, hot_ref):
    lane = lax.broadcasted_iota(jnp.int32, (128, 128), 1).astype(F32)
    for side, ref in enumerate((up_ref, down_ref)):
        index = ref[...].astype(F32)
        frequency = jnp.floor((index + 0.5) * (1.0 / ND))
        index = (index - ND * frequency) * NF + frequency
        index = jnp.transpose(jnp.concatenate([index, jnp.zeros((128 - TILES, 128), F32)], axis=0))
        for r in range(TILES):
            column_ref[side, r * 128 : r * 128 + 128, :] = jnp.broadcast_to(index[:, r : r + 1], (128, 128))
    for t in range(TILES):
        for side in range(2):
            tile = (t + side) % TILES
            index = [column_ref[side, pl.ds(4 * tile + i, NF, stride=ND), :] for i in range(4)]
            index = jnp.concatenate(index, axis=0) - 128.0 * t
            index = jnp.where(index < 0.0, index + NB, index)
            both = [(index == lane + 128.0 * half).astype(F32).astype(BF16) for half in range(2)]
            hot_ref[t, side * 128 : side * 128 + 128, :] = jnp.concatenate(both, axis=1)


def sources(field, wind_x, wind_y, wet, tab_ref, hot_ref, round_ref, pair_ref, delta_ref, add_ref):
    total = jnp.zeros((128, 128), F32)
    for t in range(TILES):
        f = field[:, lanes(t)]
        round_ref[:, lanes(t)] = f.astype(BF16)
        scaled = f * tab_ref[RATE : RATE + 1, lanes(t)]
        total = total + scaled * scaled
    round_ref[:, lanes(TILES)] = round_ref[:, lanes(0)]
    steep = jnp.sqrt(jnp.sum(total, axis=1, keepdims=True) * (1.0 / NB) + 1e-06)
    steep = jnp.broadcast_to(steep, (128, 128))

    def gather(t):
        both = lax.dot_general(
            round_ref[:, lanes(t, 2)], hot_ref[t], (((1,), (1,)), ((), ())), preferred_element_type=F32
        )
        pair_ref[0, :, lanes(t)] = both[:, :128]
        pair_ref[1, :, lanes((t + 1) % TILES)] = both[:, 128:]

    for t in range(TILES):
        gather(t)

    def combine(t):
        f = field[:, lanes(t)]
        plus, minus = pair_ref[0, :, lanes(t)], pair_ref[1, :, lanes(t)]
        row = lambda r: tab_ref[r : r + 1, lanes(t)]
        delta = (row(DELTA) * f) * (
            f * (PLUS_WEIGHT * plus + MINUS_WEIGHT * minus) - (2.0 * BOTH_WEIGHT) * plus * minus
        )
        delta_ref[:, lanes(t)] = delta.astype(BF16)
        growth = jnp.maximum(wind_x * row(GROW_X) + wind_y * row(GROW_Y) - row(GROW_0), 0.0)
        field[:, lanes(t)] = f + growth * f - (row(DAMP) * steep) * f - 2.0 * delta

    for t in range(TILES):
        combine(t)
    delta_ref[:, lanes(TILES)] = delta_ref[:, lanes(0)]

    def scatter(t):
        back = jnp.dot(delta_ref[:, lanes(t, 2)], hot_ref[t], preferred_element_type=F32)
        add_ref[0, :, lanes(t)] = back[:, :128]
        add_ref[1, :, lanes((t + 1) % TILES)] = back[:, 128:]

    for t in range(TILES):
        scatter(t)

    def finish(t):
        field[:, lanes(t)] = wet * (field[:, lanes(t)] + add_ref[0, :, lanes(t)] + add_ref[1, :, lanes(t)])

    for t in range(TILES):
        finish(t)


def move_rows(src, part, shift, tab_ref):
    for t in range(TILES):
        f = src[:, lanes(t)]
        high = f.astype(BF16)
        low = (f - high.astype(F32)).astype(BF16)
        moved = jnp.dot(shift, jnp.concatenate([high, low], axis=0), preferred_element_type=F32)
        row = lambda r: tab_ref[r : r + 1, lanes(t)]
        part[:, lanes(t)] = row(KEEP) * f + row(MOVE_UP) * moved[:128] + row(MOVE_DOWN) * moved[128:]


def move_columns(g, part, dst, west, east, edges, rows, wet, tab_ref):
    at = chunk(g)
    lane = lax.broadcasted_iota(jnp.int32, (32, 128), 1)
    top, bottom, here = rows[at, :] == 0.0, rows[at, :] == float(NW - 1), wet[at, :]
    for t in range(TILES):
        cols = slice(t * 128, t * 128 + 128)
        row = lambda r: tab_ref[r : r + 1, cols]
        if t < 4:
            near_y = west[at, cols]
        elif t > 4:
            near_y = east[at, (t - 4) * 128 : (t - 3) * 128]
        else:
            near_y = jnp.where(lane < SPLIT - 512, west[at, cols], east[at, 0:128])
        above = jnp.where(top, row(MOVE_UP) * edges[0:1, cols], 0.0)
        below = jnp.where(bottom, row(MOVE_DOWN) * edges[8:9, cols], 0.0)
        dst[at, cols] = here * (part[at, cols] + above + below + row(MOVE_Y) * near_y)


def to_bins(last, out):
    for t in range(TILES):
        block = jnp.transpose(last[:, t * 128 : t * 128 + 128])
        for i in range(4):
            out[pl.ds(4 * t + i, NF, stride=ND), :] = block[i * NF : (i + 1) * NF]


def kernel(
    spectrum_in,
    speed_in,
    direction_in,
    wet_in,
    order_in,
    up_in,
    down_in,
    tab_in,
    last,
    spectrum,
    speed,
    direction,
    wet_ref,
    order_ref,
    up_ref,
    down_ref,
    tab_ref,
    load,
    index_ref,
    first,
    second,
    part,
    wind_row,
    wind_all,
    west,
    east,
    edge_out,
    edge_in,
    rows_ref,
    col_wet_ref,
    hot,
    rounded,
    pair,
    delta,
    add,
    spare,
    spare_w,
    send_a,
    recv_a,
    send_w,
    recv_w,
    send_h,
    recv_h,
    send_e,
    recv_e,
    send_b,
    recv_b,
):
    me = lax.axis_index("wide")
    strip = lax.axis_index("sub")
    plane, z, y = me // 8, lax.rem(me, 8), me // 32
    column = column_of(me)
    lower, upper = column > 0, column < NW - 1
    to_lower, to_upper = device_of(jnp.maximum(column - 1, 0)), device_of(jnp.minimum(column + 1, NW - 1))
    has_above, has_below = strip > 0, strip < NS - 1
    one = lambda ref, i: ref.at[pl.ds(i, 1)]

    for k in range(2):
        for is_there, blank in (
            (lower, west.at[k]),
            (upper, east.at[k]),
            (has_above, edge_in.at[k, 0:8]),
            (has_below, edge_in.at[k, 8:16]),
        ):

            @pl.when(jnp.logical_not(is_there))
            def _(blank=blank):
                blank[...] = jnp.zeros(blank.shape, F32)

    barrier = pltpu.get_barrier_semaphore()
    line_peer = lambda i: plane * 8 + lax.rem(z + i, 8)
    plane_peer = lambda i: lax.rem(plane + i, 16) * 8 + z

    def greet(peer, sem):
        def signal(i, carry):
            pl.semaphore_signal(sem, inc=1, device_id={"wide": peer(i)}, device_id_type=MESH)
            return carry

        return signal

    lax.fori_loop(1, NW, greet(lambda i: lax.rem(me + i, NW), barrier), 0)

    @pl.when(has_above)
    def _():
        pl.semaphore_signal(barrier, inc=1, device_id={"sub": strip - 1}, device_id_type=MESH)

    @pl.when(has_below)
    def _():
        pl.semaphore_signal(barrier, inc=1, device_id={"sub": strip + 1}, device_id_type=MESH)

    inputs = (
        (up_in, up_ref),
        (down_in, down_ref),
        (speed_in, speed),
        (direction_in, direction),
        (wet_in, wet_ref),
        (order_in, order_ref),
        (tab_in, tab_ref),
        (spectrum_in, spectrum),
    )
    inputs = [pltpu.make_async_copy(src, dst, load.at[i]) for i, (src, dst) in enumerate(inputs)]
    for copy in inputs:
        copy.start()
    for copy in inputs[:-1]:
        copy.wait()

    row_ids = lax.broadcasted_iota(jnp.int32, (128, 128), 0).astype(F32)
    lane_ids = lax.broadcasted_iota(jnp.int32, (128, 128), 1).astype(F32)
    ones = jnp.ones((128, 128), BF16)
    order = order_ref[...].astype(F32)
    rows = spread(order)
    rows_ref[...] = rows
    wet_grid = wet_ref[...].astype(F32)
    mine = jnp.sum(jnp.where(lane_ids == me.astype(F32), order, 0.0), axis=1, keepdims=True)
    own_wet = jnp.where(row_ids == mine, wet_grid, 0.0).astype(BF16)
    own_wet = lax.dot_general(own_wet, ones, (((0,), (0,)), ((), ())), preferred_element_type=F32)
    col_wet = jnp.where(lane_ids == column.astype(F32), wet_grid, 0.0).astype(BF16)
    col_wet = jnp.dot(col_wet, ones, preferred_element_type=F32).astype(BF16)
    pick = (lane_ids == rows).astype(F32).astype(BF16)
    col_wet_ref[...] = jnp.dot(pick, col_wet, preferred_element_type=F32)
    above_hot = (order == rows - 1.0).astype(F32)
    below_hot = (order == rows + 1.0).astype(F32)
    shift = jnp.concatenate([above_hot, below_hot], axis=0)
    shift = jnp.concatenate([shift, shift], axis=1).astype(BF16)

    wind_x = speed[...] * jnp.cos(direction[...])
    wind_y = speed[...] * jnp.sin(direction[...])
    wind_row[0:1, 0:128] = wind_x
    wind_row[0:1, 128:256] = wind_y
    build_partners(up_ref, down_ref, index_ref, hot)
    inputs[-1].wait()
    for t in range(TILES):
        block = jnp.concatenate([spectrum[pl.ds(4 * t + i, NF, stride=ND), :] for i in range(4)], axis=0)
        first[:, t * 128 : t * 128 + 128] = jnp.transpose(block)
    sources(first, spread(wind_x), spread(wind_y), own_wet, tab_ref, hot, rounded, pair, delta, add)

    beside = has_above.astype(jnp.int32) + has_below.astype(jnp.int32)
    pl.semaphore_wait(barrier, NW - 1 + beside)

    pltpu.make_async_copy(one(wind_row, 0), one(wind_all, me), recv_w.at[0]).start()
    pltpu.make_async_copy(one(wind_row, 0), one(spare_w, 0), send_w.at[0]).start()

    def send_line(i, carry):
        pltpu.make_async_remote_copy(
            one(wind_row, 0),
            one(wind_all, me),
            send_w.at[0],
            recv_w.at[0],
            device_id={"wide": line_peer(i)},
            device_id_type=MESH,
        ).start()
        return carry

    lax.fori_loop(1, 8, send_line, 0)

    pltpu.make_async_copy(one(first, column), one(second, me), recv_a.at[y]).start()
    pltpu.make_async_copy(one(first, column), one(spare, 0), send_a).start()

    def send_out(i, carry):
        w = lax.rem(me + i, NW)
        pltpu.make_async_remote_copy(
            one(first, column_of(w)),
            one(second, me),
            send_a,
            recv_a.at[y],
            device_id={"wide": w},
            device_id_type=MESH,
        ).start()
        return carry

    lax.fori_loop(1, NW, send_out, 0)

    wind_line = wind_all.at[chunk(plane, 8)]
    pltpu.make_async_copy(wind_line, wind_line, recv_w.at[0]).wait()

    def send_plane(i, carry):
        pltpu.make_async_remote_copy(
            wind_line,
            wind_line,
            send_w.at[1],
            recv_w.at[1],
            device_id={"wide": plane_peer(i)},
            device_id_type=MESH,
        ).start()
        return carry

    lax.fori_loop(1, 16, send_plane, 0)

    def side_copies(k, field):
        def west_copy(g):
            return pltpu.make_async_remote_copy(
                field.at[chunk(g), 0:HALF],
                west.at[k, chunk(g)],
                send_h.at[k, 0, g],
                recv_h.at[k, 0, g],
                device_id={"wide": to_upper},
                device_id_type=MESH,
            )

        def east_copy(g):
            return pltpu.make_async_remote_copy(
                field.at[chunk(g), NB - HALF : NB],
                east.at[k, chunk(g)],
                send_h.at[k, 1, g],
                recv_h.at[k, 1, g],
                device_id={"wide": to_lower},
                device_id_type=MESH,
            )

        return west_copy, east_copy

    def edge_copies(k):
        return [
            (
                sends,
                gets,
                pltpu.make_async_remote_copy(
                    edge_out.at[k, pl.ds(8 * i, 1)],
                    edge_in.at[k, pl.ds(8 * i, 1)],
                    send_e.at[k, i],
                    recv_e.at[k, i],
                    device_id={"sub": to},
                    device_id_type=MESH,
                ),
            )
            for i, sends, gets, to in (
                (0, has_below, has_above, jnp.minimum(strip + 1, NS - 1)),
                (1, has_above, has_below, jnp.maximum(strip - 1, 0)),
            )
        ]

    def start_edges(k, field):
        rows = rows_ref[...]

        for t in range(TILES):
            f = field[:, lanes(t)]
            edge_out[k, 0:1, lanes(t)] = jnp.sum(jnp.where(rows == float(NW - 1), f, 0.0), axis=0, keepdims=True)
            edge_out[k, 8:9, lanes(t)] = jnp.sum(jnp.where(rows == 0.0, f, 0.0), axis=0, keepdims=True)

        for sends, gets, copy in edge_copies(k):
            pl.when(sends)(copy.start)

    def end_edges(k):
        for sends, gets, copy in edge_copies(k):
            pl.when(gets)(copy.wait_recv)
            pl.when(sends)(copy.wait_send)

    west_copy, east_copy = side_copies(0, second)
    west_copy_1, east_copy_1 = side_copies(1, first)

    def pass_on(j, carry):
        g = lax.rem(y + 3 - j, 4)
        pltpu.make_async_copy(second.at[chunk(g)], second.at[chunk(g)], recv_a.at[g]).wait()
        pl.when(upper)(lambda: west_copy(g).start())
        pl.when(lower)(lambda: east_copy(g).start())
        return carry

    lax.fori_loop(0, 4, pass_on, 0)
    start_edges(0, second)
    pltpu.make_async_copy(first, first, send_a).wait()
    move_rows(second, part, shift, tab_ref)
    end_edges(0)

    def first_columns(j, carry):
        g = lax.rem(y + 3 - j, 4)
        pl.when(lower)(lambda: west_copy(g).wait_recv())
        pl.when(upper)(lambda: east_copy(g).wait_recv())
        move_columns(g, part, first, west.at[0], east.at[0], edge_in.at[0], rows_ref, col_wet_ref, tab_ref)
        return carry

    lax.fori_loop(0, 4, first_columns, 0)

    def sent_columns(k):
        west_copy, east_copy = side_copies(k, (second, first)[k])

        def sent(g, carry):
            pl.when(upper)(lambda: west_copy(g).wait_send())
            pl.when(lower)(lambda: east_copy(g).wait_send())
            return carry

        lax.fori_loop(0, 4, sent, 0)

    others = wind_all.at[pl.ds(0, 120)]
    pltpu.make_async_copy(others, others, recv_w.at[1]).wait()
    here = lane_ids == column.astype(F32)
    wind_x, wind_y = (
        jnp.broadcast_to(
            jnp.sum(jnp.where(here, wind_all[:, i * 128 : i * 128 + 128], 0.0), axis=1, keepdims=True), (128, 128)
        )
        for i in range(2)
    )
    sources(first, wind_x, wind_y, col_wet_ref[...], tab_ref, hot, rounded, pair, delta, add)
    start_edges(1, first)
    y_upper, y_lower = to_upper // 32, to_lower // 32

    def start_columns(j, carry):
        pl.when(upper)(lambda: west_copy_1(lax.rem(y_upper + 1 + j, 4)).start())
        pl.when(lower)(lambda: east_copy_1(lax.rem(y_lower + 1 + j, 4)).start())
        return carry

    lax.fori_loop(0, 4, start_columns, 0)
    sent_columns(0)
    move_rows(first, part, shift, tab_ref)
    end_edges(1)

    def last_columns(j, carry):
        g = lax.rem(y + 1 + j, 4)
        pl.when(lower)(lambda: west_copy_1(g).wait_recv())
        pl.when(upper)(lambda: east_copy_1(g).wait_recv())
        move_columns(g, part, second, west.at[1], east.at[1], edge_in.at[1], rows_ref, col_wet_ref, tab_ref)

        def send_back(i, carry):
            w = g * 32 + lax.rem(me + i, 32)
            pltpu.make_async_remote_copy(
                one(second, w), one(last, column), send_b, recv_b, device_id={"wide": w}, device_id_type=MESH
            ).start()
            return carry

        return lax.fori_loop(j // 3, 32, send_back, carry)

    lax.fori_loop(0, 4, last_columns, 0)
    pltpu.make_async_copy(one(second, me), one(last, column), recv_b).start()
    pltpu.make_async_copy(one(second, me), one(spare, 8), send_b).start()
    sent_columns(1)
    pltpu.make_async_copy(wind_all.at[chunk(0, 8)], wind_all.at[chunk(0, 8)], send_w.at[0]).wait()
    pltpu.make_async_copy(others, others, send_w.at[1]).wait()
    pltpu.make_async_copy(last, last, recv_b).wait()
    pltpu.make_async_copy(second, second, send_b).wait()


def local(spectrum, wind_speed, wind_dir, wet_mask, row_block, plus_index, minus_index):
    dma, i32 = pltpu.SemaphoreType.DMA, jnp.int32
    vmem = lambda *shape, dtype=F32: pltpu.VMEM(shape, dtype)
    wide = NB + 128
    received = pl.pallas_call(
        kernel,
        out_shape=jax.ShapeDtypeStruct((128, NB), F32),
        in_specs=[pl.BlockSpec(memory_space=pl.ANY)] * 8,
        out_specs=pl.BlockSpec(memory_space=pltpu.VMEM),
        scratch_shapes=[
            vmem(NB, 128),
            vmem(1, 128),
            vmem(1, 128),
            vmem(128, 128, dtype=i32),
            vmem(1, 128, dtype=i32),
            vmem(TILES, 128, dtype=i32),
            vmem(TILES, 128, dtype=i32),
            vmem(16, NB),
            dma((8,)),
            vmem(2, NB, 128),
            vmem(128, NB),
            vmem(128, NB),
            vmem(128, NB),
            vmem(8, 256),
            vmem(128, 256),
            vmem(2, 128, HALF),
            vmem(2, 128, HALF),
            vmem(2, 16, NB),
            vmem(2, 16, NB),
            vmem(128, 128),
            vmem(128, 128),
            vmem(TILES, 256, 256, dtype=BF16),
            vmem(128, wide, dtype=BF16),
            vmem(2, 128, NB),
            vmem(128, wide, dtype=BF16),
            vmem(2, 128, NB),
            vmem(16, NB),
            vmem(8, 256),
            dma,
            dma((4,)),
            dma((2,)),
            dma((2,)),
            dma((2, 2, 4)),
            dma((2, 2, 4)),
            dma((2, 2)),
            dma((2, 2)),
            dma,
            dma,
        ],
        compiler_params=pltpu.CompilerParams(
            collective_id=0, has_side_effects=True, vmem_limit_bytes=60 * 2**20
        ),
    )(
        spectrum,
        wind_speed.reshape(1, 128),
        wind_dir.reshape(1, 128),
        wet_mask,
        row_block,
        plus_index.reshape(TILES, 128),
        minus_index.reshape(TILES, 128),
        jnp.asarray(bin_table()),
    )
    return pl.pallas_call(to_bins, out_shape=jax.ShapeDtypeStruct((NB, 128), F32))(received)


def solution(mesh):
    placed = (
        P(None, ("wide", "sub")),
        P(("wide", "sub")),
        P(("wide", "sub")),
        P("sub", None),
        P("sub", None),
        P(),
        P(),
    )
    return jax.shard_map(
        local, mesh=mesh, in_specs=placed, out_specs=P(None, ("wide", "sub")), check_vma=False
    )
```

time: 120 us -> 94.5 us (0.79)
  local copies, waits for them, and re-layouts: 15 us -> 0 us
  Pallas kernels: 104 us -> 94.3 us
    gather x2 -> x0, local copies, waits for them, and re-layouts: 13 us -> none  [local(): up, down = (turned(plus_index)[old], turned(minus_index)[old])]
    pallas_call x1 -> x2, Pallas kernels: 104 us -> 94.3 us  [the longest x1 92.2 us: local(): pl.pallas_call(kernel, out_shape=jax.ShapeDtypeStruct((128, NB), F32), in...]
    unnamed x17 -> x0, local copies, waits for them, and re-layouts: 2.04 us -> none
where the time goes in v2:
time: 94.5 us; the launch traced here: 94.3 us
  Pallas kernels  94.3 us (100%)
    pallas_call x1, Pallas kernels, local(): pl.pallas_call(kernel, out_shape=jax.ShapeDtypeStruct((128, NB), F32), in...  92.2 us
    pallas_call x1, Pallas kernels, local(): pl.pallas_call(to_bins, out_shape=jax.ShapeDtypeStruct((NB, 128), F32))  2.11 us

profile of v2, /device:TPU:1, one launch (start us, length us, event | category | flops | bytes accessed | tf_op | source)
XLA Modules:
  0.0 94.3 jit_solution(2098702724545762350)
XLA Ops:
  0.0 92.2 %shard_map.82.last = f32[128,1152]{1,0:T(8,128)} custom-call(f32[1152,128]{1,0:T(8,128)} %spectrum_in.1, f32[1,128]{1,0:T(1,128)} %bitcast.6, f32[1,128]{1,0:T(1,128)} %bitcast.7, s32[128,128]{1,0:T(8,128)} %wet_in.1, s32[1,128]{1,0:T(1,128)} %order_in.1, s32[9,128]{1,0:T(8,128)} %bitcast.4, s32[9,128]{1,0:T(8,128)} %bitcast.5, f32[16,1152]{1,0:T(8,128)} %constant.2.clone.tab_in), custom_call_target="tpu_custom_call" | custom-call | tf_op jit(solution)/shard_map/pallas_call | solution.py:530
  92.2 2.1 %shard_map.83 = f32[1152,128]{1,0:T(8,128)} custom-call(f32[128,1152]{1,0:T(8,128)} %shard_map.82.last), custom_call_target="tpu_custom_call" | custom-call | tf_op jit(solution)/shard_map/pallas_call | solution.py:588

commit v3 on v2

--- a/solution.py
+++ b/solution.py
@@ -55,8 +55,10 @@
     return table
 
 
-def column_of(w):
+def column_of(w, strip):
+    w = lax.rem(w + 32 * lax.rem(strip, 2), NW)
     plane, z = w // 8, lax.rem(w, 8)
+    z = z + (strip // 2) * (7 - 2 * z)
     y, x = plane // 4, lax.rem(plane, 4)
     turn = lax.rem(y, 2)
     p = y * 4 + x + turn * (3 - 2 * x)
@@ -64,14 +66,15 @@
     return z * 16 + p + back * (15 - 2 * p)
 
 
-def device_of(c):
+def device_of(c, strip):
     z, q = c // 16, lax.rem(c, 16)
     back = lax.rem(z, 2)
     p = q + back * (15 - 2 * q)
     y, i = p // 4, lax.rem(p, 4)
     turn = lax.rem(y, 2)
     x = i + turn * (3 - 2 * i)
-    return (y * 4 + x) * 8 + z
+    z = z + (strip // 2) * (7 - 2 * z)
+    return lax.rem((y * 4 + x) * 8 + z + 96 * lax.rem(strip, 2), NW)
 
 
 def lanes(t, count=1):
@@ -244,9 +247,11 @@
     me = lax.axis_index("wide")
     strip = lax.axis_index("sub")
     plane, z, y = me // 8, lax.rem(me, 8), me // 32
-    column = column_of(me)
+    column = column_of(me, strip)
     lower, upper = column > 0, column < NW - 1
-    to_lower, to_upper = device_of(jnp.maximum(column - 1, 0)), device_of(jnp.minimum(column + 1, NW - 1))
+    to_lower, to_upper = device_of(jnp.maximum(column - 1, 0), strip), device_of(jnp.minimum(column + 1, NW - 1), strip)
+    to_above = device_of(column, jnp.maximum(strip - 1, 0))
+    to_below = device_of(column, jnp.minimum(strip + 1, NS - 1))
     has_above, has_below = strip > 0, strip < NS - 1
     one = lambda ref, i: ref.at[pl.ds(i, 1)]
 
@@ -277,11 +282,11 @@
 
     @pl.when(has_above)
     def _():
-        pl.semaphore_signal(barrier, inc=1, device_id={"sub": strip - 1}, device_id_type=MESH)
+        pl.semaphore_signal(barrier, inc=1, device_id={"wide": to_above, "sub": strip - 1}, device_id_type=MESH)
 
     @pl.when(has_below)
     def _():
-        pl.semaphore_signal(barrier, inc=1, device_id={"sub": strip + 1}, device_id_type=MESH)
+        pl.semaphore_signal(barrier, inc=1, device_id={"wide": to_below, "sub": strip + 1}, device_id_type=MESH)
 
     inputs = (
         (up_in, up_ref),
@@ -348,16 +353,16 @@
 
     lax.fori_loop(1, 8, send_line, 0)
 
-    pltpu.make_async_copy(one(first, column), one(second, me), recv_a.at[y]).start()
+    pltpu.make_async_copy(one(first, column), one(second, me), recv_a.at[plane]).start()
     pltpu.make_async_copy(one(first, column), one(spare, 0), send_a).start()
 
     def send_out(i, carry):
         w = lax.rem(me + i, NW)
         pltpu.make_async_remote_copy(
-            one(first, column_of(w)),
+            one(first, column_of(w, strip)),
             one(second, me),
             send_a,
-            recv_a.at[y],
+            recv_a.at[plane],
             device_id={"wide": w},
             device_id_type=MESH,
         ).start()
@@ -414,13 +419,13 @@
                     edge_in.at[k, pl.ds(8 * i, 1)],
                     send_e.at[k, i],
                     recv_e.at[k, i],
-                    device_id={"sub": to},
+                    device_id=to,
                     device_id_type=MESH,
                 ),
             )
             for i, sends, gets, to in (
-                (0, has_below, has_above, jnp.minimum(strip + 1, NS - 1)),
-                (1, has_above, has_below, jnp.maximum(strip - 1, 0)),
+                (0, has_below, has_above, {"wide": to_below, "sub": jnp.minimum(strip + 1, NS - 1)}),
+                (1, has_above, has_below, {"wide": to_above, "sub": jnp.maximum(strip - 1, 0)}),
             )
         ]
 
@@ -440,40 +445,65 @@
             pl.when(gets)(copy.wait_recv)
             pl.when(sends)(copy.wait_send)
 
-    west_copy, east_copy = side_copies(0, second)
     west_copy_1, east_copy_1 = side_copies(1, first)
 
+    first_sides = (
+        (
+            upper,
+            lower,
+            lambda g: pltpu.make_async_remote_copy(
+                second.at[chunk(g, 8), 0:HALF],
+                west.at[0, chunk(g, 8)],
+                send_h.at[0, 0, 0],
+                recv_h.at[0, 0, 0],
+                device_id={"wide": to_upper},
+                device_id_type=MESH,
+            ),
+            west.at[0],
+        ),
+        (
+            lower,
+            upper,
+            lambda g: pltpu.make_async_remote_copy(
+                second.at[chunk(g, 8), NB - HALF : NB],
+                east.at[0, chunk(g, 8)],
+                send_h.at[0, 1, 0],
+                recv_h.at[0, 1, 0],
+                device_id={"wide": to_lower},
+                device_id_type=MESH,
+            ),
+            east.at[0],
+        ),
+    )
+
     def pass_on(j, carry):
-        g = lax.rem(y + 3 - j, 4)
-        pltpu.make_async_copy(second.at[chunk(g)], second.at[chunk(g)], recv_a.at[g]).wait()
-        pl.when(upper)(lambda: west_copy(g).start())
-        pl.when(lower)(lambda: east_copy(g).start())
+        g = lax.rem(plane + 15 - j, 16)
+        pltpu.make_async_copy(second.at[chunk(g, 8)], second.at[chunk(g, 8)], recv_a.at[g]).wait()
+        for sends, gets, copy, landed in first_sides:
+            pl.when(jnp.logical_and(sends, j < 15))(lambda copy=copy: copy(g).start())
         return carry
 
-    lax.fori_loop(0, 4, pass_on, 0)
+    lax.fori_loop(0, 16, pass_on, 0)
     start_edges(0, second)
+    for sends, gets, copy, landed in first_sides:
+        pl.when(sends)(lambda copy=copy: copy(plane).start())
     pltpu.make_async_copy(first, first, send_a).wait()
     move_rows(second, part, shift, tab_ref)
     end_edges(0)
 
-    def first_columns(j, carry):
-        g = lax.rem(y + 3 - j, 4)
-        pl.when(lower)(lambda: west_copy(g).wait_recv())
-        pl.when(upper)(lambda: east_copy(g).wait_recv())
+    for i, (sends, gets, copy, landed) in enumerate(first_sides):
+        pl.when(gets)(pltpu.make_async_copy(landed, landed, recv_h.at[0, i, 0]).wait)
+
+    def first_columns(g, carry):
         move_columns(g, part, first, west.at[0], east.at[0], edge_in.at[0], rows_ref, col_wet_ref, tab_ref)
         return carry
 
     lax.fori_loop(0, 4, first_columns, 0)
 
-    def sent_columns(k):
-        west_copy, east_copy = side_copies(k, (second, first)[k])
-
-        def sent(g, carry):
-            pl.when(upper)(lambda: west_copy(g).wait_send())
-            pl.when(lower)(lambda: east_copy(g).wait_send())
-            return carry
-
-        lax.fori_loop(0, 4, sent, 0)
+    def sent_columns(g, carry):
+        pl.when(upper)(lambda: west_copy_1(g).wait_send())
+        pl.when(lower)(lambda: east_copy_1(g).wait_send())
+        return carry
 
     others = wind_all.at[pl.ds(0, 120)]
     pltpu.make_async_copy(others, others, recv_w.at[1]).wait()
@@ -489,17 +519,18 @@
     y_upper, y_lower = to_upper // 32, to_lower // 32
 
     def start_columns(j, carry):
-        pl.when(upper)(lambda: west_copy_1(lax.rem(y_upper + 1 + j, 4)).start())
-        pl.when(lower)(lambda: east_copy_1(lax.rem(y_lower + 1 + j, 4)).start())
+        pl.when(upper)(lambda: west_copy_1(lax.rem(y_upper + j, 4)).start())
+        pl.when(lower)(lambda: east_copy_1(lax.rem(y_lower + j, 4)).start())
         return carry
 
     lax.fori_loop(0, 4, start_columns, 0)
-    sent_columns(0)
+    for i, (sends, gets, copy, landed) in enumerate(first_sides):
+        pl.when(sends)(pltpu.make_async_copy(landed, landed, send_h.at[0, i, 0]).wait)
     move_rows(first, part, shift, tab_ref)
     end_edges(1)
 
     def last_columns(j, carry):
-        g = lax.rem(y + 1 + j, 4)
+        g = lax.rem(y + j, 4)
         pl.when(lower)(lambda: west_copy_1(g).wait_recv())
         pl.when(upper)(lambda: east_copy_1(g).wait_recv())
         move_columns(g, part, second, west.at[1], east.at[1], edge_in.at[1], rows_ref, col_wet_ref, tab_ref)
@@ -511,12 +542,12 @@
             ).start()
             return carry
 
-        return lax.fori_loop(j // 3, 32, send_back, carry)
+        return lax.fori_loop((3 - j) // 3, 32, send_back, carry)
 
     lax.fori_loop(0, 4, last_columns, 0)
     pltpu.make_async_copy(one(second, me), one(last, column), recv_b).start()
     pltpu.make_async_copy(one(second, me), one(spare, 8), send_b).start()
-    sent_columns(1)
+    lax.fori_loop(0, 4, sent_columns, 0)
     pltpu.make_async_copy(wind_all.at[chunk(0, 8)], wind_all.at[chunk(0, 8)], send_w.at[0]).wait()
     pltpu.make_async_copy(others, others, send_w.at[1]).wait()
     pltpu.make_async_copy(last, last, recv_b).wait()
@@ -562,7 +593,7 @@
             vmem(16, NB),
             vmem(8, 256),
             dma,
-            dma((4,)),
+            dma((16,)),
             dma((2,)),
             dma((2,)),
             dma((2, 2, 4)),

time: 94.5 us -> 91.7 us (0.970)
  Pallas kernels: 94.3 us -> 91.5 us
    pallas_call x1, Pallas kernels: 92.2 us -> 89.4 us  [local(): pl.pallas_call(kernel, out_shape=jax.ShapeDtypeStruct((128, NB), F32), in...]
where the time goes in v3:
time: 91.7 us; the launch traced here: 91.5 us
  Pallas kernels  91.5 us (100%)
    pallas_call x1, Pallas kernels, local(): pl.pallas_call(kernel, out_shape=jax.ShapeDtypeStruct((128, NB), F32), in...  89.4 us
    pallas_call x1, Pallas kernels, local(): pl.pallas_call(to_bins, out_shape=jax.ShapeDtypeStruct((NB, 128), F32))  2.11 us

profile of v3, /device:TPU:1, one launch (start us, length us, event | category | flops | bytes accessed | tf_op | source)
XLA Modules:
  0.0 91.5 jit_solution(7535624410749854940)
XLA Ops:
  0.0 89.4 %shard_map.82.last = f32[128,1152]{1,0:T(8,128)} custom-call(f32[1152,128]{1,0:T(8,128)} %spectrum_in.1, f32[1,128]{1,0:T(1,128)} %bitcast.6, f32[1,128]{1,0:T(1,128)} %bitcast.7, s32[128,128]{1,0:T(8,128)} %wet_in.1, s32[1,128]{1,0:T(1,128)} %order_in.1, s32[9,128]{1,0:T(8,128)} %bitcast.4, s32[9,128]{1,0:T(8,128)} %bitcast.5, f32[16,1152]{1,0:T(8,128)} %constant.2.clone.tab_in), custom_call_target="tpu_custom_call" | custom-call | tf_op jit(solution)/shard_map/pallas_call | solution.py:561
  89.4 2.1 %shard_map.83 = f32[1152,128]{1,0:T(8,128)} custom-call(f32[128,1152]{1,0:T(8,128)} %shard_map.82.last), custom_call_target="tpu_custom_call" | custom-call | tf_op jit(solution)/shard_map/pallas_call | solution.py:619

commit v4 on v3

--- a/solution.py
+++ b/solution.py
@@ -487,12 +487,13 @@
     start_edges(0, second)
     for sends, gets, copy, landed in first_sides:
         pl.when(sends)(lambda copy=copy: copy(plane).start())
-    pltpu.make_async_copy(first, first, send_a).wait()
     move_rows(second, part, shift, tab_ref)
     end_edges(0)
 
     for i, (sends, gets, copy, landed) in enumerate(first_sides):
         pl.when(gets)(pltpu.make_async_copy(landed, landed, recv_h.at[0, i, 0]).wait)
+
+    pltpu.make_async_copy(first, first, send_a).wait()
 
     def first_columns(g, carry):
         move_columns(g, part, first, west.at[0], east.at[0], edge_in.at[0], rows_ref, col_wet_ref, tab_ref)
@@ -524,10 +525,10 @@
         return carry
 
     lax.fori_loop(0, 4, start_columns, 0)
+    move_rows(first, part, shift, tab_ref)
+    end_edges(1)
     for i, (sends, gets, copy, landed) in enumerate(first_sides):
         pl.when(sends)(pltpu.make_async_copy(landed, landed, send_h.at[0, i, 0]).wait)
-    move_rows(first, part, shift, tab_ref)
-    end_edges(1)
 
     def last_columns(j, carry):
         g = lax.rem(y + j, 4)

time: 91.7 us -> 91.7 us (level)
  no operation moved by 1% of the time
where the time goes in v4:
time: 91.7 us; the launch traced here: 91.5 us
  Pallas kernels  91.5 us (100%)
    pallas_call x1, Pallas kernels, local(): pl.pallas_call(kernel, out_shape=jax.ShapeDtypeStruct((128, NB), F32), in...  89.4 us
    pallas_call x1, Pallas kernels, local(): pl.pallas_call(to_bins, out_shape=jax.ShapeDtypeStruct((NB, 128), F32))  2.11 us

profile of v4, /device:TPU:1, one launch (start us, length us, event | category | flops | bytes accessed | tf_op | source)
XLA Modules:
  0.0 91.5 jit_solution(8189101828710624001)
XLA Ops:
  0.0 89.4 %shard_map.82.last = f32[128,1152]{1,0:T(8,128)} custom-call(f32[1152,128]{1,0:T(8,128)} %spectrum_in.1, f32[1,128]{1,0:T(1,128)} %bitcast.6, f32[1,128]{1,0:T(1,128)} %bitcast.7, s32[128,128]{1,0:T(8,128)} %wet_in.1, s32[1,128]{1,0:T(1,128)} %order_in.1, s32[9,128]{1,0:T(8,128)} %bitcast.4, s32[9,128]{1,0:T(8,128)} %bitcast.5, f32[16,1152]{1,0:T(8,128)} %constant.2.clone.tab_in), custom_call_target="tpu_custom_call" | custom-call | tf_op jit(solution)/shard_map/pallas_call | solution.py:562
  89.4 2.1 %shard_map.83 = f32[1152,128]{1,0:T(8,128)} custom-call(f32[128,1152]{1,0:T(8,128)} %shard_map.82.last), custom_call_target="tpu_custom_call" | custom-call | tf_op jit(solution)/shard_map/pallas_call | solution.py:620
